TPU v7x, 512 devices: a whole 4x4x16 slice. The times are simulated.
512 devices in a mesh: dp: 8 (over y, core), table: 64 (over x, z).
Axes of the slice: x: 4, y: 4, z: 16, core: 2. Of those that a mesh axis runs over, the one named last changes fastest.
Arguments:
- item_table: bfloat16 [16384, 512], P('table'), may hold values from -6 to 6
- input_weight: bfloat16 [512, 2048], replicated, may hold values from -0.25 to 0.25
- output_weight: bfloat16 [512, 512], replicated, may hold values from -0.25 to 0.25
- request_rows: int32 [512, 64, 4], P(('dp', 'table')), may hold values from 0 to 255
- negative_rows: int32 [512, 64, 1], P(('dp', 'table')), may hold values from 0 to 255
- token_slots: int32 [512, 128], P(('dp', 'table')), may hold values from 0 to 255, as said below
- history_lengths: int32 [512, 4], P(('dp', 'table')), may hold values from 1 to 64, 128 in all within a row
Outputs:
- losses: float32 [65536], P(('dp', 'table'))
- table_grad: float32 [16384, 512], P('table', 'dp')
Inputs may be any that keep to these rules, and one draw needn't show every extreme that they name: token_slots points only to live slots: slot s of device d's list to shard o is live when s is below that pair's live count, which is 1 to 4; in every draw one shard receives 4 live slots from every device.
All inputs are finite; a program needn't handle non-finite values.
Results may differ from a plain program's by a relative error of at most 0.014.
Values may be sent and summed in bfloat16 or wider, within the bound.
A program may use at most 64 MiB of HBM per device.

v0:
```python
import jax
import jax.numpy as jnp
from jax import lax
from jax.sharding import PartitionSpec as P

HEADS = 4
HEAD = 128
MAXLEN = 64
CAP = 4
NEG_OWN = 1


TEMPER = 0.05


def unit_rows(values):
    return values * lax.rsqrt(jnp.sum(values * values, axis=-1, keepdims=True) + 1e-06)


def center(values):
    middle = jnp.mean(values, axis=-1, keepdims=True)
    spread = values - middle
    return spread * lax.rsqrt(jnp.mean(spread * spread, axis=-1, keepdims=True) + 1e-05)


def layer_loss(inputs, negatives, lengths_row, input_weight, output_weight):
    rows_here = inputs.shape[0]
    normed = center(inputs).astype(jnp.bfloat16)
    mixed = jax.nn.silu(jnp.dot(normed, input_weight, preferred_element_type=jnp.float32)).astype(
        jnp.bfloat16
    )
    gate, values, queries, keys_all = jnp.split(mixed, 4, axis=1)
    ends = jnp.cumsum(lengths_row)
    where_at = jnp.arange(rows_here, dtype=jnp.int32)
    segment = jnp.sum((where_at[:, None] >= ends[None, :]).astype(jnp.int32), axis=1)
    allowed = (segment[:, None] == segment[None, :]) & (where_at[None, :] <= where_at[:, None])
    query_h = queries.reshape(rows_here, HEADS, HEAD)
    key_h = keys_all.reshape(rows_here, HEADS, HEAD)
    value_h = values.reshape(rows_here, HEADS, HEAD)
    scores = jnp.einsum("qhd,khd->hqk", query_h, key_h, preferred_element_type=jnp.float32)
    weights = jnp.where(allowed[None], jax.nn.silu(scores * HEAD ** (-0.5)), 0.0) / MAXLEN
    weights = weights.astype(jnp.bfloat16)
    attended = jnp.einsum("hqk,khd->qhd", weights, value_h, preferred_element_type=jnp.float32)
    attended = attended.reshape(rows_here, HEADS * HEAD)
    gated = (center(attended) * gate.astype(jnp.float32)).astype(jnp.bfloat16)
    outputs = jnp.dot(gated, output_weight, preferred_element_type=jnp.float32) + inputs
    unit_out = unit_rows(outputs).astype(jnp.bfloat16)
    unit_items = unit_rows(inputs).astype(jnp.bfloat16)
    unit_negs = unit_rows(negatives).astype(jnp.bfloat16)
    target = jnp.concatenate([unit_items[1:], jnp.zeros_like(unit_items[:1])], axis=0)
    positive = jnp.sum(unit_out.astype(jnp.float32) * target.astype(jnp.float32), axis=1) / TEMPER
    negative = (
        lax.dot_general(
            unit_out, unit_negs, (((1,), (1,)), ((), ())), preferred_element_type=jnp.float32
        )
        / TEMPER
    )
    total = jnp.exp(positive) + jnp.sum(jnp.exp(negative), axis=1)
    valid = jnp.concatenate([segment[1:] == segment[:-1], jnp.zeros((1,), dtype=bool)])
    return jnp.where(valid, jnp.log(total) - positive, 0.0)


def body(
    item_table,
    input_weight,
    output_weight,
    request_rows,
    negative_rows,
    token_slots,
    history_lengths,
):
    shards = request_rows.shape[1]
    width = item_table.shape[1]
    asks = jnp.concatenate([request_rows[0], negative_rows[0]], axis=1)
    asked = lax.all_to_all(asks, "table", split_axis=0, concat_axis=0, tiled=True)
    found = item_table[asked]
    fetched = lax.all_to_all(found, "table", split_axis=0, concat_axis=0, tiled=True)
    history = fetched[:, :CAP].reshape(shards * CAP, width)
    own_negs = fetched[:, CAP:].reshape(shards * NEG_OWN, width)
    scored = lax.all_gather(own_negs, "dp", axis=0, tiled=True)
    slots = token_slots[0]
    inputs = history[slots].astype(jnp.float32)

    def local(first, second):
        return layer_loss(first, second, history_lengths[0], input_weight, output_weight)

    device_losses, pullback = jax.vjp(local, inputs, scored.astype(jnp.float32))
    grad_inputs, grad_negs = pullback(jnp.ones_like(device_losses))
    slot_grads = jnp.zeros((shards * CAP, width), jnp.float32).at[slots].add(grad_inputs)
    slot_grads = slot_grads.reshape(shards, CAP, width)
    mine = lax.psum_scatter(
        grad_negs.astype(jnp.bfloat16), "dp", scatter_dimension=0, tiled=True
    ).astype(jnp.float32)
    outgoing = jnp.concatenate([slot_grads, mine.reshape(shards, NEG_OWN, width)], axis=1)
    arrived = lax.all_to_all(outgoing, "table", split_axis=0, concat_axis=0, tiled=True)
    shard_grad = jnp.zeros((item_table.shape[0], width), jnp.float32)
    shard_grad = shard_grad.at[asked.reshape(-1)].add(arrived.reshape(-1, width))
    table_grad = lax.psum_scatter(shard_grad, "dp", scatter_dimension=1, tiled=True)
    return (device_losses, table_grad)


def solution(mesh):
    placed = (
        P("table", None),
        P(),
        P(),
        P(("dp", "table"), None, None),
        P(("dp", "table"), None, None),
        P(("dp", "table"), None),
        P(("dp", "table"), None),
    )
    return jax.shard_map(
        body,
        mesh=mesh,
        in_specs=placed,
        out_specs=(P(("dp", "table")), P("table", "dp")),
        check_vma=False,
    )
```

profile of v0, /device:TPU:1, one launch (start us, length us, event | category | flops | bytes accessed | tf_op | source)
XLA Modules:
  0.0 257.4 jit_solution(5574657639626021793)
XLA Ops:
  8.1 32.2 %all_to_all.22 = s32[64,1,5]{2,1,0:T(1,128)S(1)} all-to-all(s32[64,1,5]{2,1,0:T(1,128)S(1)} %bitcast.98), channel_id=1, replica_groups=mesh['dp'=8,'table'=64] {'table'}, dimensions={0} | all-to-all | bytes 2560 | tf_op jit(solution)/shard_map/all_to_all | solution.py:75
  41.1 3.0 %gather_fusion = bf16[320,512]{1,0:T(8,128)(2,1)S(1)} fusion(bf16[256,512]{1,0:T(8,128)(2,1)} %param.7, s32[1024]{0:T(1024)S(1)} %pad_clamp_fusion.1), kind=kCustom, calls=%fused_computation | custom fusion | bytes 656640 | tf_op jit(solution)/shard_map/gather | solution.py:76
  45.1 4.6 %all-to-all-start.1 = ((bf16[64,5,512]{2,1,0:T(8,128)(2,1)}), bf16[64,5,512]{2,1,0:T(8,128)(2,1)S(1)}, u32[]{:S(2)}, u32[]{:S(2)}) async-start(bf16[64,5,512]{2,1,0:T(8,128)(2,1)} %reshape.312), calls=%async_computation.1 | async-start | bytes 1048576 | tf_op jit(solution)/shard_map/all_to_all | solution.py:77
  51.9 25.9 %all-to-all-done.1 = bf16[64,5,512]{2,1,0:T(8,128)(2,1)S(1)} async-done(((bf16[64,5,512]{2,1,0:T(8,128)(2,1)}), bf16[64,5,512]{2,1,0:T(8,128)(2,1)S(1)}, u32[]{:S(2)}, u32[]{:S(2)}) %all-to-all-start.1) | async-done | bytes 327712 | tf_op jit(solution)/shard_map/all_to_all | solution.py:77
  80.6 18.1 %all-gather = bf16[512,1,512]{2,0,1:T(8,128)(2,1)S(1)} all-gather(bf16[64,1,512]{2,0,1:T(8,128)(2,1)S(1)} %copy.80), channel_id=2, replica_groups=mesh['dp'=8,'table'=64] {'dp'}, dimensions={0}, use_global_device_ids=true | all-gather | bytes 589824 | tf_op jit(solution)/shard_map/all_gather | solution.py:80
  99.2 1.5 multiply_convert_fusion
  103.1 1.1 copy.93
  104.2 1.5 multiply_reduce_fusion.2
  107.7 1.2 add_multiply_fusion
  113.0 1.0 fusion.12
  114.0 2.1 copy.99
  116.2 1.1 fusion.94
  117.3 1.0 fusion.46
  118.3 1.1 fusion.95
  119.9 2.2 fusion.37
  122.4 2.5 scatter_custom_fusion
  124.8 1.2 reshape.305
  126.1 18.7 %reduce-scatter.7.cloned.1.call-done = bf16[64,512]{1,0:T(8,128)(2,1)} async-done(((bf16[512,512]{1,0:T(8,128)(2,1)}), bf16[64,512]{1,0:T(8,128)(2,1)}) %reduce-scatter.7.cloned.1.call-update) | async-done | bytes 65552 | tf_op jit(solution)/shard_map/reduce_scatter | solution.py:91
  145.7 1.2 pad_maximum_fusion
  146.9 14.3 %all-to-all-start.2 = ((f32[64,5,512]{2,1,0:T(8,128)}), f32[64,5,512]{2,1,0:T(8,128)S(1)}, u32[]{:S(2)}, u32[]{:S(2)}) async-start(f32[64,5,512]{2,1,0:T(8,128)} %pad_maximum_fusion), calls=%async_computation.2 | async-start | bytes 2097152 | tf_op jit(solution)/shard_map/all_to_all | solution.py:95
  162.8 46.0 %all-to-all-done.2 = f32[64,5,512]{2,1,0:T(8,128)S(1)} async-done(((f32[64,5,512]{2,1,0:T(8,128)}), f32[64,5,512]{2,1,0:T(8,128)S(1)}, u32[]{:S(2)}, u32[]{:S(2)}) %all-to-all-start.2) | async-done | bytes 655392 | tf_op jit(solution)/shard_map/all_to_all | solution.py:95
  209.8 3.1 %scatter_custom_fusion.1 = f32[256,512]{1,0:T(8,128)S(1)} fusion(s32[320]{0:T(512)S(1)} %fusion.81, f32[320,512]{1,0:T(8,128)} %reshape.339, f32[]{:T(128)} %constant.23.clone.1), kind=kCustom, calls=%fused_computation.96 | custom fusion | flops 163840 | bytes 524800 | tf_op jit(solution)/shard_map/scatter-add | solution.py:97
  212.9 1.0 copy.101
  213.9 36.7 %reduce-scatter.9.cloned.1.call-done = f32[64,256]{1,0:T(8,128)} async-done(((f32[512,256]{1,0:T(8,128)}), f32[64,256]{1,0:T(8,128)}) %reduce-scatter.9.cloned.1.call-update) | async-done | bytes 65552
  (142 shorter events, 20.3 us)
Async XLA Ops:
  7.2 92.0 %copy-start = (bf16[512,2048]{1,0:T(8,128)(2,1)S(1)}, bf16[512,2048]{1,0:T(8,128)(2,1)}, u32[]{:S(2)}) copy-start(bf16[512,2048]{1,0:T(8,128)(2,1)} %param.8) | copy-start | bytes 6291460
  41.1 8.7 %copy-start.36 = (s32[1,4]{1,0:T(1,128)S(1)}, s32[1,4]{1,0:T(1,128)}, u32[]{:S(2)}) copy-start(s32[1,4]{1,0:T(1,128)} %param.13) | copy-start | bytes 52
  41.1 8.9 %copy-start.37 = (s32[1,128]{1,0:T(1,128)S(1)}, s32[1,128]{1,0:T(1,128)}, u32[]{:S(2)}) copy-start(s32[1,128]{1,0:T(1,128)} %param.12) | copy-start | bytes 1540
  45.1 32.7 %all-to-all-start.1 = ((bf16[64,5,512]{2,1,0:T(8,128)(2,1)}), bf16[64,5,512]{2,1,0:T(8,128)(2,1)S(1)}, u32[]{:S(2)}, u32[]{:S(2)}) async-start(bf16[64,5,512]{2,1,0:T(8,128)(2,1)} %reshape.312), calls=%async_computation.1 | async-start | bytes 1048576 | tf_op jit(solution)/shard_map/all_to_all | solution.py:77
  49.7 95.0 %reduce-scatter.7.cloned.1.call-start = ((), (), s32[]{:S(2)}) async-start(), calls=%async_computation.5 | async-start | bytes 589824 | tf_op jit(solution)/shard_map/reduce_scatter | solution.py:91
  80.0 20.7 %copy-start.28 = (f32[128]{0:T(128)}, f32[128]{0:T(128)S(1)}, u32[]{:S(2)}) copy-start(f32[128]{0:T(128)S(1)} %get-tuple-element.12) | copy-start | bytes 1540
  80.0 20.7 %copy-start.30 = (f32[128]{0:T(128)}, f32[128]{0:T(128)S(1)}, u32[]{:S(2)}) copy-start(f32[128]{0:T(128)S(1)} %get-tuple-element.13) | copy-start | bytes 1540
  80.0 20.7 %copy-start.23 = (f32[128]{0:T(128)}, f32[128]{0:T(128)S(1)}, u32[]{:S(2)}) copy-start(f32[128]{0:T(128)S(1)} %fusion.83) | copy-start | bytes 1540
  80.0 20.7 %copy-start.32 = (f32[128]{0:T(128)}, f32[128]{0:T(128)S(1)}, u32[]{:S(2)}) copy-start(f32[128]{0:T(128)S(1)} %add_rsqrt_fusion.1) | copy-start | bytes 1540
  99.2 2.9 %copy-start.17 = (pred[128,128]{1,0:T(8,128)(4,1)S(1)}, pred[128,128]{1,0:T(8,128)(4,1)}, u32[]{:S(2)}) copy-start(pred[128,128]{1,0:T(8,128)(4,1)} %fusion.80) | copy-start | bytes 49156
  101.8 3.9 %copy-start.8 = (f32[128,512]{1,0:T(8,128)S(1)}, f32[128,512]{1,0:T(8,128)}, u32[]{:S(2)}) copy-start(f32[128,512]{1,0:T(8,128)} %convert_element_type.107) | copy-start | bytes 786436
  105.7 4.1 %copy-start.21 = (f32[128]{0:T(128)}, f32[128]{0:T(128)S(1)}, u32[]{:S(2)}) copy-start(f32[128]{0:T(128)S(1)} %add_rsqrt_fusion.2) | copy-start | bytes 1540
  107.3 2.5 copy-start.1
  107.3 2.5 copy-start.7
  112.0 4.1 %copy-start.5 = (bf16[128,512]{0,1:T(8,128)(2,1)S(1)}, bf16[128,512]{0,1:T(8,128)(2,1)}, u32[]{:S(2)}) copy-start(bf16[128,512]{0,1:T(8,128)(2,1)} %copy-done.4) | copy-start | bytes 393220
  113.0 4.3 %copy-start.20 = (f32[128]{0:T(128)S(1)}, f32[128]{0:T(128)}, u32[]{:S(2)}) copy-start(f32[128]{0:T(128)} %copy-done.19) | copy-start | bytes 1540
  113.0 5.3 %copy-start.3 = (bf16[128,512]{0,1:T(8,128)(2,1)S(1)}, bf16[128,512]{0,1:T(8,128)(2,1)}, u32[]{:S(2)}) copy-start(bf16[128,512]{0,1:T(8,128)(2,1)} %copy-done.2) | copy-start | bytes 393220
  114.0 5.4 %copy-start.14 = (bf16[4,128,128]{2,1,0:T(8,128)(2,1)S(1)}, bf16[4,128,128]{2,1,0:T(8,128)(2,1)}, u32[]{:S(2)}) copy-start(bf16[4,128,128]{2,1,0:T(8,128)(2,1)} %convolution_convert_fusion.4) | copy-start | bytes 393220
  119.8 2.3 copy-start.24
  119.8 2.5 copy-start.22
  119.9 2.5 copy-start.26
  126.0 35.8 %copy-start.11 = (s32[64,1,5]{2,1,0:T(1,128)S(1)}, s32[64,1,5]{2,1,0:T(1,128)}, u32[]{:S(2)}) copy-start(s32[64,1,5]{2,1,0:T(1,128)} %copy-done.10) | copy-start | bytes 3844
  146.9 62.0 %all-to-all-start.2 = ((f32[64,5,512]{2,1,0:T(8,128)}), f32[64,5,512]{2,1,0:T(8,128)S(1)}, u32[]{:S(2)}, u32[]{:S(2)}) async-start(f32[64,5,512]{2,1,0:T(8,128)} %pad_maximum_fusion), calls=%async_computation.2 | async-start | bytes 2097152 | tf_op jit(solution)/shard_map/all_to_all | solution.py:95
  161.2 89.4 %reduce-scatter.9.cloned.1.call-start = ((), (), s32[]{:S(2)}) async-start(), calls=%async_computation.6 | async-start | bytes 589824
  (18 other events, 24.7 us)
Sparse Core Ops, SparseCore 0:
  116.3 28.4 reduce-scatter.6
  214.0 36.5 reduce-scatter.8
where the time goes:
time: 259 us; the launch traced here: 257 us
  waiting for transfers between devices  127 us (49%)
  blocking collectives  50.3 us (19%)
  starting transfers between devices  19.1 us (7%)
  other arithmetic  17.9 us (7%)
  local copies, waits for them, and re-layouts  16.8 us (6%)
  between operations  14.7 us (6%)
  matrix products  11.4 us (4%)
    all_to_all x1, waiting for transfers between devices, body(): lax.all_to_all(outgoing, 'table', split_axis=0, concat_axis=0, tiled=True)  46 us
    unnamed x3, waiting for transfers between devices  36.7 us
    all_to_all x1, blocking collectives, body(): lax.all_to_all(asks, 'table', split_axis=0, concat_axis=0, tiled=True)  32.2 us
    all_to_all x1, waiting for transfers between devices, body(): lax.all_to_all(found, 'table', split_axis=0, concat_axis=0, tiled=True)  25.9 us
    reduce_scatter x1, waiting for transfers between devices, body(): lax.psum_scatter(grad_negs.astype(jnp.bfloat16), 'dp', scatter_dimension=...  18.7 us
    all_gather x1, blocking collectives, body(): scored = lax.all_gather(own_negs, 'dp', axis=0, tiled=True)  18.1 us
    all_to_all x1, starting transfers between devices, body(): lax.all_to_all(outgoing, 'table', split_axis=0, concat_axis=0, tiled=True)  14.3 us
    unnamed x78, local copies, waits for them, and re-layouts  5.23 us
  transfers between devices with their start and end apart: 4, of which 4 were waited for; matrix products, arithmetic and copies ran while one was open for 5% of the time, Pallas kernels for 0%

commit v1 on v0

v1 whole, which is shorter than its diff:
```python
import jax
import jax.numpy as jnp
from jax import lax
from jax.experimental import pallas as pl
from jax.experimental.pallas import tpu as pltpu
from jax.sharding import PartitionSpec as P

MESH = pl.DeviceIdType.MESH
BF16 = jnp.bfloat16
F32 = jnp.float32

N_DP = 8
N_TABLE = 64
Z_RING = 16
X_RING = 4
D = 512
HEADS = 4
HEAD = 128
TOK = 128
MAXLEN = 64
CAP = 4
OWN_ITEMS = 256
NEGS = N_DP * N_TABLE
LANES = 128
CHUNKS = D // LANES
TEMPER = 0.05


def dot(a, b, contract=((1,), (0,))):
    return lax.dot_general(a, b, (contract, ((), ())), preferred_element_type=F32)


def rows_to_slabs(value, slab, slots):
    for s in range(slots):
        for c in range(CHUNKS):
            slab[pl.ds(s * CHUNKS + c, N_TABLE, stride=slots * CHUNKS), :] = value[
                s * N_TABLE : (s + 1) * N_TABLE, c * LANES : (c + 1) * LANES
            ]


def slabs_to_rows(slab, slots):
    rows = []
    for s in range(slots):
        parts = [
            slab[pl.ds(s * CHUNKS + c, N_TABLE, stride=slots * CHUNKS), :]
            for c in range(CHUNKS)
        ]
        rows.append(jnp.concatenate(parts, axis=1))
    return rows[0] if slots == 1 else jnp.concatenate(rows, axis=0)


def center_parts(values):
    middle = jnp.mean(values, axis=-1, keepdims=True)
    spread = values - middle
    scale = lax.rsqrt(jnp.mean(spread * spread, axis=-1, keepdims=True) + 1e-05)
    return spread * scale, scale


def center_back(grad, normed, scale):
    first = jnp.mean(grad, axis=-1, keepdims=True)
    second = jnp.mean(grad * normed, axis=-1, keepdims=True)
    return scale * (grad - first - normed * second)


def unit_scale(values):
    return lax.rsqrt(jnp.sum(values * values, axis=-1, keepdims=True) + 1e-06)


def unit_back(grad, values, scale):
    along = jnp.sum(grad * values, axis=-1, keepdims=True)
    return scale * grad - values * (scale * scale * scale * along)


def kernel(
    table_hbm,
    in_weight_hbm,
    out_weight_hbm,
    request_ref,
    negative_ref,
    token_ref,
    length_ref,
    loss_ref,
    grad_ref,
    table_v,
    in_weight,
    out_weight,
    ask_src,
    ask_dst,
    picks,
    picks_t,
    slab_rows,
    slab_negs,
    row_src,
    row_dst,
    neg_src,
    neg_dst,
    unit_all,
    neg_raw,
    neg_out,
    neg_in,
    back_src,
    back_dst,
    neg_back_src,
    neg_back_dst,
    shard_src,
    shard_dst,
    local_sem,
    send_sem,
    recv_sem,
):
    i = lax.axis_index("dp")
    t = lax.axis_index("table")
    tx, tz = t // Z_RING, lax.rem(t, Z_RING)

    def table_peer(k):
        return lax.rem(tx + lax.rem(k, X_RING), X_RING) * Z_RING + lax.rem(
            tz + k // X_RING, Z_RING
        )

    loads = [
        pltpu.make_async_copy(src, dst, local_sem.at[n])
        for n, (src, dst) in enumerate(
            ((table_hbm, table_v), (in_weight_hbm, in_weight), (out_weight_hbm, out_weight))
        )
    ]
    for load in loads:
        load.start()

    barrier = pltpu.get_barrier_semaphore()

    def greet(k, carry):
        pl.semaphore_signal(
            barrier, inc=1, device_id={"table": table_peer(k)}, device_id_type=MESH
        )
        return carry

    lax.fori_loop(1, N_TABLE, greet, 0)
    for k in range(1, N_DP):
        pl.semaphore_signal(
            barrier, inc=1, device_id={"dp": lax.rem(i + k, N_DP)}, device_id_type=MESH
        )

    def send_table(src, dst, n):
        def step(k, carry):
            peer = table_peer(k)
            pltpu.make_async_remote_copy(
                src_ref=src.at[peer],
                dst_ref=dst.at[t],
                send_sem=send_sem.at[n],
                recv_sem=recv_sem.at[n],
                device_id={"table": peer},
                device_id_type=MESH,
            ).start()
            return carry

        lax.fori_loop(1, N_TABLE, step, 0)

    def send_dp(src_of, dst, n):
        for k in range(1, N_DP):
            peer = lax.rem(i + k, N_DP)
            pltpu.make_async_remote_copy(
                src_ref=src_of(peer),
                dst_ref=dst,
                send_sem=send_sem.at[n],
                recv_sem=recv_sem.at[n],
                device_id={"dp": peer},
                device_id_type=MESH,
            ).start()

    def wait_all(ref, count, n):
        part = ref.at[pl.ds(0, count)]
        pltpu.make_async_copy(part, part, recv_sem.at[n]).wait()

    def wait_sent(ref, count, n):
        part = ref.at[pl.ds(0, count)]
        pltpu.make_async_copy(part, part, send_sem.at[n]).wait()

    lane = lax.broadcasted_iota(jnp.int32, (N_TABLE, LANES), 1)
    asks = jnp.zeros((N_TABLE, LANES), jnp.int32)
    for s in range(CAP):
        asks = jnp.where(lane == s, request_ref[0, :, s : s + 1], asks)
    asks = jnp.where(lane == CAP, negative_ref[0, :, 0:1], asks)
    ask_src[:, 0, :] = asks
    ask_dst[pl.ds(t, 1)] = ask_src[pl.ds(t, 1)]
    pl.semaphore_wait(barrier, N_TABLE - 1 + N_DP - 1)
    send_table(ask_src, ask_dst, 0)

    sub_tok = lax.broadcasted_iota(jnp.int32, (TOK, TOK), 0)
    lane_tok = lax.broadcasted_iota(jnp.int32, (TOK, TOK), 1)
    seg_q = jnp.zeros((TOK, TOK), jnp.int32)
    seg_k = jnp.zeros((TOK, TOK), jnp.int32)
    seg_next = jnp.zeros((TOK, TOK), jnp.int32)
    end = jnp.int32(0)
    for n in range(length_ref.shape[1]):
        end = end + length_ref[0, n]
        seg_q = seg_q + (sub_tok >= end).astype(jnp.int32)
        seg_k = seg_k + (lane_tok >= end).astype(jnp.int32)
        seg_next = seg_next + (sub_tok + 1 >= end).astype(jnp.int32)
    allowed = (seg_q == seg_k) & (lane_tok <= sub_tok)
    valid = ((seg_q == seg_next) & (sub_tok < TOK - 1))[:, 0:1]
    slots = token_ref[...]
    place = (slots & (CAP - 1)) * N_TABLE + slots // CAP
    token_t = (
        lax.broadcasted_iota(jnp.int32, (CAP * N_TABLE, TOK), 0) == place
    ).astype(F32)
    token_pick = jnp.transpose(token_t).astype(BF16)
    token_t = token_t.astype(BF16)

    loads[0].wait()
    wait_all(ask_dst, N_TABLE - 1, 0)
    asked = ask_dst[:, 0, :]
    item = lax.broadcasted_iota(jnp.int32, (N_TABLE, OWN_ITEMS), 1)
    for s in range(CAP + 1):
        picks[s * N_TABLE : (s + 1) * N_TABLE, :] = (
            (asked[:, s : s + 1] == item).astype(F32).astype(BF16)
        )
    own_table = table_v[...]
    found_negs = dot(picks[CAP * N_TABLE :, :], own_table)
    for c in range(CHUNKS):
        slab_negs[:, c, :] = found_negs[:, c * LANES : (c + 1) * LANES]
    neg_src[...] = slab_negs[...].astype(BF16)
    neg_dst[pl.ds(t, 1)] = neg_src[pl.ds(t, 1)]
    send_table(neg_src, neg_dst, 1)
    rows_to_slabs(dot(picks[: CAP * N_TABLE, :], own_table), slab_rows, CAP)
    row_src[...] = slab_rows[...].astype(BF16).reshape(row_src.shape)
    row_dst[pl.ds(t, 1)] = row_src[pl.ds(t, 1)]
    send_table(row_src, row_dst, 2)
    picks_t[...] = jnp.transpose(picks[...].astype(F32)).astype(BF16)

    wait_all(neg_dst, N_TABLE - 1, 1)
    slab_negs[...] = neg_dst[...].astype(F32)
    negs = jnp.concatenate([slab_negs[:, c, :] for c in range(CHUNKS)], axis=1)
    neg_raw[...] = negs
    unit_all[pl.ds(i, 1)] = (negs * unit_scale(negs)).astype(BF16)[None]
    send_dp(lambda peer: unit_all.at[i], unit_all.at[i], 3)
    loads[1].wait()
    loads[2].wait()

    wait_all(row_dst, N_TABLE - 1, 2)
    slab_rows[...] = row_dst[...].reshape(slab_rows.shape).astype(F32)
    history = slabs_to_rows(slab_rows, CAP).astype(BF16)
    inputs = dot(token_pick, history)
    normed, in_scale = center_parts(inputs)
    pre = dot(normed.astype(BF16), in_weight[...])
    sig = jax.nn.sigmoid(pre)
    mixed = (pre * sig).astype(BF16)
    gate, values, queries, keys = (mixed[:, n * D : (n + 1) * D] for n in range(4))
    raw, weights, attended = [], [], []
    for h in range(HEADS):
        at = slice(h * HEAD, (h + 1) * HEAD)
        scores = dot(queries[:, at], keys[:, at], ((1,), (1,))) * HEAD ** (-0.5)
        raw.append(scores)
        weight = jnp.where(allowed, scores * jax.nn.sigmoid(scores), 0.0) / MAXLEN
        weights.append(weight.astype(BF16))
        attended.append(dot(weights[h], values[:, at]))
    att_normed, att_scale = center_parts(jnp.concatenate(attended, axis=1))
    gate32 = gate.astype(F32)
    gated = (att_normed * gate32).astype(BF16)
    outputs = dot(gated, out_weight[...]) + inputs
    out_scale = unit_scale(outputs)
    unit_out = (outputs * out_scale).astype(BF16)
    item_scale = unit_scale(inputs)
    unit_items = (inputs * item_scale).astype(BF16).astype(F32)
    target = pltpu.roll(unit_items, TOK - 1, 0)
    unit_out32 = unit_out.astype(F32)
    positive = jnp.sum(unit_out32 * target, axis=1, keepdims=True) / TEMPER

    wait_all(unit_all, N_DP - 1, 3)
    unit_negs = unit_all[...].reshape(NEGS, D)
    exp_neg = jnp.exp(dot(unit_out, unit_negs, ((1,), (1,))) / TEMPER)
    exp_pos = jnp.exp(positive)
    total = exp_pos + jnp.sum(exp_neg, axis=1, keepdims=True)
    loss = jnp.where(valid, jnp.log(total) - positive, 0.0)
    loss_ref[...] = jnp.transpose(jnp.broadcast_to(loss, (TOK, LANES)))[0:1, :]

    per_row = jnp.where(valid, 1.0 / (total * TEMPER), 0.0)
    d_neg = (exp_neg * per_row).astype(BF16)
    d_pos = jnp.where(valid, exp_pos * per_row - 1.0 / TEMPER, 0.0)
    neg_out[...] = dot(d_neg, unit_out, ((0,), (0,))).astype(BF16).reshape(neg_out.shape)
    send_dp(lambda peer: neg_out.at[peer], neg_in.at[i], 4)
    neg_in[pl.ds(i, 1)] = neg_out[pl.ds(i, 1)]

    d_unit_out = dot(d_neg, unit_negs) + d_pos * target
    d_outputs = unit_back(d_unit_out, outputs, out_scale)
    d_unit_items = pltpu.roll(d_pos * unit_out32, 1, 0)
    d_inputs = d_outputs + unit_back(d_unit_items, inputs, item_scale)

    d_gated = dot(d_outputs.astype(BF16), out_weight[...], ((1,), (1,)))
    d_gate = d_gated * att_normed
    d_att = center_back(d_gated * gate32, att_normed, att_scale).astype(BF16)
    d_values, d_queries, d_keys = [], [], []
    for h in range(HEADS):
        at = slice(h * HEAD, (h + 1) * HEAD)
        d_weight = dot(d_att[:, at], values[:, at], ((1,), (1,)))
        d_values.append(dot(weights[h], d_att[:, at], ((0,), (0,))))
        s_sig = jax.nn.sigmoid(raw[h])
        slope = s_sig * (1.0 + raw[h] * (1.0 - s_sig))
        d_scores = jnp.where(
            allowed, d_weight * slope * (HEAD ** (-0.5) / MAXLEN), 0.0
        ).astype(BF16)
        d_queries.append(dot(d_scores, keys[:, at]))
        d_keys.append(dot(d_scores, queries[:, at], ((0,), (0,))))
    d_mixed = jnp.concatenate([d_gate] + d_values + d_queries + d_keys, axis=1)
    d_pre = (d_mixed * (sig * (1.0 + pre * (1.0 - sig)))).astype(BF16)
    d_normed = dot(d_pre, in_weight[...], ((1,), (1,)))
    d_inputs = d_inputs + center_back(d_normed, normed, in_scale)

    wait_all(neg_in, N_DP - 1, 4)
    d_units = jnp.sum(neg_in[...].astype(F32), axis=0)
    own_negs = neg_raw[...]
    d_negs = unit_back(d_units, own_negs, unit_scale(own_negs))
    for c in range(CHUNKS):
        slab_negs[:, c, :] = d_negs[:, c * LANES : (c + 1) * LANES]
    neg_back_src[...] = slab_negs[...].astype(BF16)
    neg_back_dst[pl.ds(t, 1)] = neg_back_src[pl.ds(t, 1)]
    send_table(neg_back_src, neg_back_dst, 5)

    rows_to_slabs(dot(token_t, d_inputs.astype(BF16)), slab_rows, CAP)
    back_src[...] = slab_rows[...].astype(BF16).reshape(back_src.shape)
    back_dst[pl.ds(t, 1)] = back_src[pl.ds(t, 1)]
    send_table(back_src, back_dst, 6)

    wait_all(neg_back_dst, N_TABLE - 1, 5)
    slab_negs[...] = neg_back_dst[...].astype(F32)
    back_negs = jnp.concatenate([slab_negs[:, c, :] for c in range(CHUNKS)], axis=1)
    shard_negs = dot(picks_t[:, CAP * N_TABLE :], back_negs.astype(BF16))
    wait_all(back_dst, N_TABLE - 1, 6)
    slab_rows[...] = back_dst[...].reshape(slab_rows.shape).astype(F32)
    back_rows = slabs_to_rows(slab_rows, CAP).astype(BF16)
    shard = shard_negs + dot(picks_t[:, : CAP * N_TABLE], back_rows)

    half = OWN_ITEMS // 2
    left = lax.broadcasted_iota(jnp.int32, (half, LANES), 1) < LANES // 2
    for c in range(CHUNKS):
        top = shard[:half, c * LANES : (c + 1) * LANES]
        low = shard[half:, c * LANES : (c + 1) * LANES]
        top_r, low_r = pltpu.roll(top, LANES // 2, 1), pltpu.roll(low, LANES // 2, 1)
        shard_src[2 * c] = jnp.where(left, top, low_r).astype(BF16)
        shard_src[2 * c + 1] = jnp.where(left, top_r, low).astype(BF16)
    send_dp(lambda peer: shard_src.at[peer], shard_dst.at[i], 7)
    shard_dst[pl.ds(i, 1)] = shard_src[pl.ds(i, 1)]

    wait_sent(ask_src, N_TABLE - 1, 0)
    wait_sent(neg_src, N_TABLE - 1, 1)
    wait_sent(row_src, N_TABLE - 1, 2)
    wait_sent(unit_all, N_DP - 1, 3)
    wait_sent(neg_out, N_DP - 1, 4)
    wait_sent(neg_back_src, N_TABLE - 1, 5)
    wait_sent(back_src, N_TABLE - 1, 6)
    wait_sent(shard_src, N_DP - 1, 7)
    wait_all(shard_dst, N_DP - 1, 7)
    summed = jnp.sum(shard_dst[...].astype(F32), axis=0)
    grad_ref[:half, :] = summed[:, : LANES // 2]
    grad_ref[half:, :] = pltpu.roll(summed, LANES // 2, 1)[:, : LANES // 2]


def body(
    item_table,
    input_weight,
    output_weight,
    request_rows,
    negative_rows,
    token_slots,
    history_lengths,
):
    vmem = pl.BlockSpec(memory_space=pltpu.VMEM)
    smem = pl.BlockSpec(memory_space=pltpu.SMEM)
    anywhere = pl.BlockSpec(memory_space=pl.ANY)
    loss, grad = pl.pallas_call(
        kernel,
        name="hstu_step",
        out_shape=(
            jax.ShapeDtypeStruct((1, TOK), F32),
            jax.ShapeDtypeStruct((OWN_ITEMS, D // N_DP), F32),
        ),
        in_specs=[anywhere, anywhere, anywhere, vmem, vmem, vmem, smem],
        out_specs=(vmem, vmem),
        scratch_shapes=[
            pltpu.VMEM((OWN_ITEMS, D), BF16),
            pltpu.VMEM((D, 4 * D), BF16),
            pltpu.VMEM((D, D), BF16),
            pltpu.VMEM((N_TABLE, 1, LANES), jnp.int32),
            pltpu.VMEM((N_TABLE, 1, LANES), jnp.int32),
            pltpu.VMEM(((CAP + 1) * N_TABLE, OWN_ITEMS), BF16),
            pltpu.VMEM((OWN_ITEMS, (CAP + 1) * N_TABLE), BF16),
            pltpu.VMEM((N_TABLE * CAP * CHUNKS, LANES), F32),
            pltpu.VMEM((N_TABLE, CHUNKS, LANES), F32),
            pltpu.VMEM((N_TABLE, CAP * CHUNKS, LANES), BF16),
            pltpu.VMEM((N_TABLE, CAP * CHUNKS, LANES), BF16),
            pltpu.VMEM((N_TABLE, CHUNKS, LANES), BF16),
            pltpu.VMEM((N_TABLE, CHUNKS, LANES), BF16),
            pltpu.VMEM((N_DP, N_TABLE, D), BF16),
            pltpu.VMEM((N_TABLE, D), F32),
            pltpu.VMEM((N_DP, N_TABLE, D), BF16),
            pltpu.VMEM((N_DP, N_TABLE, D), BF16),
            pltpu.VMEM((N_TABLE, CAP * CHUNKS, LANES), BF16),
            pltpu.VMEM((N_TABLE, CAP * CHUNKS, LANES), BF16),
            pltpu.VMEM((N_TABLE, CHUNKS, LANES), BF16),
            pltpu.VMEM((N_TABLE, CHUNKS, LANES), BF16),
            pltpu.VMEM((N_DP, OWN_ITEMS // 2, LANES), BF16),
            pltpu.VMEM((N_DP, OWN_ITEMS // 2, LANES), BF16),
            pltpu.SemaphoreType.DMA((3,)),
            pltpu.SemaphoreType.DMA((8,)),
            pltpu.SemaphoreType.DMA((8,)),
        ],
        compiler_params=pltpu.CompilerParams(
            collective_id=0, has_side_effects=True, vmem_limit_bytes=48 * 2**20
        ),
    )(
        item_table,
        input_weight,
        output_weight,
        request_rows,
        negative_rows,
        token_slots,
        history_lengths,
    )
    return loss.reshape(TOK), grad


def solution(mesh):
    placed = (
        P("table", None),
        P(),
        P(),
        P(("dp", "table"), None, None),
        P(("dp", "table"), None, None),
        P(("dp", "table"), None),
        P(("dp", "table"), None),
    )
    return jax.shard_map(
        body,
        mesh=mesh,
        in_specs=placed,
        out_specs=(P(("dp", "table")), P("table", "dp")),
        check_vma=False,
    )
```

time: 259 us -> 89.2 us (0.34)
  waiting for transfers between devices: 127 us -> 0 us
  Pallas kernels: 0 us -> 80.7 us
  blocking collectives: 50.3 us -> 0 us
  starting transfers between devices: 19.1 us -> 0 us
  other arithmetic: 17.9 us -> 0 us
  between operations: 14.7 us -> 0.64 us
  matrix products: 11.4 us -> 0 us
  local copies, waits for them, and re-layouts: 16.8 us -> 7.63 us
    pallas_call x0 -> x1, Pallas kernels: none -> 80.7 us  [body(): pl.pallas_call(kernel, name='hstu_step', out_shape=(jax.ShapeDtypeStruct(...]
    all_to_all x2 -> x0, waiting for transfers between devices: 71.9 us -> none  [the longest x1 46 us: body(): lax.all_to_all(outgoing, 'table', split_axis=0, concat_axis=0, tiled=True)]
    unnamed x3 -> x0, waiting for transfers between devices: 36.7 us -> none
    all_to_all x1 -> x0, blocking collectives: 32.2 us -> none  [body(): lax.all_to_all(asks, 'table', split_axis=0, concat_axis=0, tiled=True)]
    all_to_all x2 -> x0, starting transfers between devices: 19 us -> none  [the longest x1 14.3 us: body(): lax.all_to_all(outgoing, 'table', split_axis=0, concat_axis=0, tiled=True)]
    reduce_scatter x1 -> x0, waiting for transfers between devices: 18.7 us -> none  [body(): lax.psum_scatter(grad_negs.astype(jnp.bfloat16), 'dp', scatter_dimension=...]
    all_gather x1 -> x0, blocking collectives: 18.1 us -> none  [body(): scored = lax.all_gather(own_negs, 'dp', axis=0, tiled=True)]
    dot_general x13 -> x0, matrix products: 11.4 us -> none  [the longest x2 3.74 us: layer_loss(): jnp.dot(normed, input_weight, preferred_element_type=jnp.float32)]
  transfers between devices with their start and end apart: 4 -> 0, of which waited for: 4 -> 0; matrix products, arithmetic and copies ran while one was open for 5% -> 0% of each run, Pallas kernels for 0% -> 0%
where the time goes in v1:
time: 89.2 us; the launch traced here: 88.9 us
  Pallas kernels  80.7 us (90%)
  local copies, waits for them, and re-layouts  7.63 us (9%)
    pallas_call x1, Pallas kernels, body(): pl.pallas_call(kernel, name='hstu_step', out_shape=(jax.ShapeDtypeStruct(...  80.7 us
    unnamed x14, local copies, waits for them, and re-layouts  7.63 us

profile of v1, /device:TPU:1, one launch (start us, length us, event | category | flops | bytes accessed | tf_op | source)
XLA Modules:
  0.0 88.9 jit_solution(7089547512148884356)
XLA Ops:
  0.6 0.8 copy.9.request_ref
  1.4 0.7 copy.10.negative_ref
  2.1 0.0 copy-start
  2.1 1.6 %copy-done = bf16[512,2048]{1,0:T(8,128)(2,1)S(1)} copy-done((bf16[512,2048]{1,0:T(8,128)(2,1)S(1)}, bf16[512,2048]{1,0:T(8,128)(2,1)}, u32[]{:S(2)}) %copy-start) | copy-done | bytes 2097176
  3.7 0.0 copy-start.1
  3.7 1.0 %copy-done.1 = bf16[512,512]{1,0:T(8,128)(2,1)S(1)} copy-done((bf16[512,512]{1,0:T(8,128)(2,1)S(1)}, bf16[512,512]{1,0:T(8,128)(2,1)}, u32[]{:S(2)}) %copy-start.1) | copy-done | bytes 524312
  4.8 0.0 copy-start.2
  4.8 0.9 %copy-done.2 = bf16[256,512]{1,0:T(8,128)(2,1)S(1)} copy-done((bf16[256,512]{1,0:T(8,128)(2,1)S(1)}, bf16[256,512]{1,0:T(8,128)(2,1)}, u32[]{:S(2)}) %copy-start.2) | copy-done | bytes 262168
  5.7 0.0 copy-start.3
  5.7 0.7 copy-done.3
  6.4 0.0 copy-start.4
  6.4 0.7 copy-done.4
  7.0 80.7 %hstu_step.1 = (f32[1,128]{1,0:T(1,128)S(1)}, f32[256,64]{1,0:T(8,128)S(1)}) custom-call(bf16[256,512]{1,0:T(8,128)(2,1)S(1)} %copy-done.2, bf16[512,2048]{1,0:T(8,128)(2,1)S(1)} %copy-done, bf16[512,512]{1,0:T(8,128)(2,1)S(1)} %copy-done.1, s32[1,64,4]{2,1,0:T(8,128)S(1)} %copy.9.request_ref, s32[1,64,1]{2,1,0:T(8,128)S(1)} %copy.10.negative_ref, ...), custom_call_target="tpu_custom_call" | custom-call | tf_op jit(solution)/shard_map/hstu_step/pallas_call | solution.py:369
  87.7 0.7 copy.11
  88.4 0.5 copy.13
Async XLA Ops:
  2.1 1.6 %copy-start = (bf16[512,2048]{1,0:T(8,128)(2,1)S(1)}, bf16[512,2048]{1,0:T(8,128)(2,1)}, u32[]{:S(2)}) copy-start(bf16[512,2048]{1,0:T(8,128)(2,1)} %in_weight_hbm.1) | copy-start | bytes 6291460
  3.7 1.0 %copy-start.1 = (bf16[512,512]{1,0:T(8,128)(2,1)S(1)}, bf16[512,512]{1,0:T(8,128)(2,1)}, u32[]{:S(2)}) copy-start(bf16[512,512]{1,0:T(8,128)(2,1)} %out_weight_hbm.1) | copy-start | bytes 1572868
  4.8 0.9 %copy-start.2 = (bf16[256,512]{1,0:T(8,128)(2,1)S(1)}, bf16[256,512]{1,0:T(8,128)(2,1)}, u32[]{:S(2)}) copy-start(bf16[256,512]{1,0:T(8,128)(2,1)} %table_hbm.1) | copy-start | bytes 786436
  5.7 0.7 copy-start.3
  6.4 0.7 copy-start.4

commit v2 on v1

--- a/solution.py
+++ b/solution.py
@@ -18,12 +18,19 @@
 HEAD = 128
 TOK = 128
 MAXLEN = 64
+SEQS = 4
 CAP = 4
 OWN_ITEMS = 256
 NEGS = N_DP * N_TABLE
 LANES = 128
 CHUNKS = D // LANES
 TEMPER = 0.05
+
+
+OFFSETS = sorted(
+    ((x, z) for x in range(X_RING) for z in range(Z_RING) if x or z),
+    key=lambda o: -(min(o[0], X_RING - o[0]) + min(o[1], Z_RING - o[1])),
+)
 
 
 def dot(a, b, contract=((1,), (0,))):
@@ -72,15 +79,18 @@
 
 
 def kernel(
+    request_hbm,
+    negative_hbm,
+    token_hbm,
     table_hbm,
     in_weight_hbm,
     out_weight_hbm,
-    request_ref,
-    negative_ref,
-    token_ref,
-    length_ref,
+    length_hbm,
     loss_ref,
     grad_ref,
+    request_v,
+    token_v,
+    length_ref,
     table_v,
     in_weight,
     out_weight,
@@ -112,15 +122,21 @@
     t = lax.axis_index("table")
     tx, tz = t // Z_RING, lax.rem(t, Z_RING)
 
-    def table_peer(k):
-        return lax.rem(tx + lax.rem(k, X_RING), X_RING) * Z_RING + lax.rem(
-            tz + k // X_RING, Z_RING
-        )
+    def table_peer(offset):
+        return lax.rem(tx + offset[0], X_RING) * Z_RING + lax.rem(tz + offset[1], Z_RING)
 
     loads = [
         pltpu.make_async_copy(src, dst, local_sem.at[n])
         for n, (src, dst) in enumerate(
-            ((table_hbm, table_v), (in_weight_hbm, in_weight), (out_weight_hbm, out_weight))
+            (
+                (request_hbm, request_v.at[pl.ds(0, CAP)]),
+                (negative_hbm, request_v.at[pl.ds(CAP, 1)]),
+                (token_hbm, token_v),
+                (table_hbm, table_v),
+                (in_weight_hbm, in_weight),
+                (out_weight_hbm, out_weight),
+                (length_hbm, length_ref),
+            )
         )
     ]
     for load in loads:
@@ -128,21 +144,18 @@
 
     barrier = pltpu.get_barrier_semaphore()
 
-    def greet(k, carry):
+    for offset in OFFSETS:
         pl.semaphore_signal(
-            barrier, inc=1, device_id={"table": table_peer(k)}, device_id_type=MESH
+            barrier, inc=1, device_id={"table": table_peer(offset)}, device_id_type=MESH
         )
-        return carry
-
-    lax.fori_loop(1, N_TABLE, greet, 0)
     for k in range(1, N_DP):
         pl.semaphore_signal(
             barrier, inc=1, device_id={"dp": lax.rem(i + k, N_DP)}, device_id_type=MESH
         )
 
     def send_table(src, dst, n):
-        def step(k, carry):
-            peer = table_peer(k)
+        for offset in OFFSETS:
+            peer = table_peer(offset)
             pltpu.make_async_remote_copy(
                 src_ref=src.at[peer],
                 dst_ref=dst.at[t],
@@ -151,9 +164,6 @@
                 device_id={"table": peer},
                 device_id_type=MESH,
             ).start()
-            return carry
-
-        lax.fori_loop(1, N_TABLE, step, 0)
 
     def send_dp(src_of, dst, n):
         for k in range(1, N_DP):
@@ -175,18 +185,19 @@
         part = ref.at[pl.ds(0, count)]
         pltpu.make_async_copy(part, part, send_sem.at[n]).wait()
 
-    lane = lax.broadcasted_iota(jnp.int32, (N_TABLE, LANES), 1)
-    asks = jnp.zeros((N_TABLE, LANES), jnp.int32)
-    for s in range(CAP):
-        asks = jnp.where(lane == s, request_ref[0, :, s : s + 1], asks)
-    asks = jnp.where(lane == CAP, negative_ref[0, :, 0:1], asks)
-    ask_src[:, 0, :] = asks
+    loads[0].wait()
+    loads[1].wait()
+    asks = jnp.concatenate(
+        [request_v[0 : CAP + 1, :], jnp.zeros((LANES - CAP - 1, N_TABLE), jnp.int32)], axis=0
+    )
+    ask_src[:, 0, :] = jnp.transpose(asks.astype(F32)).astype(jnp.int32)
     ask_dst[pl.ds(t, 1)] = ask_src[pl.ds(t, 1)]
     pl.semaphore_wait(barrier, N_TABLE - 1 + N_DP - 1)
     send_table(ask_src, ask_dst, 0)
 
     sub_tok = lax.broadcasted_iota(jnp.int32, (TOK, TOK), 0)
     lane_tok = lax.broadcasted_iota(jnp.int32, (TOK, TOK), 1)
+    loads[6].wait()
     seg_q = jnp.zeros((TOK, TOK), jnp.int32)
     seg_k = jnp.zeros((TOK, TOK), jnp.int32)
     seg_next = jnp.zeros((TOK, TOK), jnp.int32)
@@ -198,7 +209,8 @@
         seg_next = seg_next + (sub_tok + 1 >= end).astype(jnp.int32)
     allowed = (seg_q == seg_k) & (lane_tok <= sub_tok)
     valid = ((seg_q == seg_next) & (sub_tok < TOK - 1))[:, 0:1]
-    slots = token_ref[...]
+    loads[2].wait()
+    slots = token_v[...]
     place = (slots & (CAP - 1)) * N_TABLE + slots // CAP
     token_t = (
         lax.broadcasted_iota(jnp.int32, (CAP * N_TABLE, TOK), 0) == place
@@ -206,7 +218,7 @@
     token_pick = jnp.transpose(token_t).astype(BF16)
     token_t = token_t.astype(BF16)
 
-    loads[0].wait()
+    loads[3].wait()
     wait_all(ask_dst, N_TABLE - 1, 0)
     asked = ask_dst[:, 0, :]
     item = lax.broadcasted_iota(jnp.int32, (N_TABLE, OWN_ITEMS), 1)
@@ -233,8 +245,8 @@
     neg_raw[...] = negs
     unit_all[pl.ds(i, 1)] = (negs * unit_scale(negs)).astype(BF16)[None]
     send_dp(lambda peer: unit_all.at[i], unit_all.at[i], 3)
-    loads[1].wait()
-    loads[2].wait()
+    loads[4].wait()
+    loads[5].wait()
 
     wait_all(row_dst, N_TABLE - 1, 2)
     slab_rows[...] = row_dst[...].reshape(slab_rows.shape).astype(F32)
@@ -305,6 +317,11 @@
     d_normed = dot(d_pre, in_weight[...], ((1,), (1,)))
     d_inputs = d_inputs + center_back(d_normed, normed, in_scale)
 
+    rows_to_slabs(dot(token_t, d_inputs.astype(BF16)), slab_rows, CAP)
+    back_src[...] = slab_rows[...].astype(BF16).reshape(back_src.shape)
+    back_dst[pl.ds(t, 1)] = back_src[pl.ds(t, 1)]
+    send_table(back_src, back_dst, 6)
+
     wait_all(neg_in, N_DP - 1, 4)
     d_units = jnp.sum(neg_in[...].astype(F32), axis=0)
     own_negs = neg_raw[...]
@@ -314,11 +331,6 @@
     neg_back_src[...] = slab_negs[...].astype(BF16)
     neg_back_dst[pl.ds(t, 1)] = neg_back_src[pl.ds(t, 1)]
     send_table(neg_back_src, neg_back_dst, 5)
-
-    rows_to_slabs(dot(token_t, d_inputs.astype(BF16)), slab_rows, CAP)
-    back_src[...] = slab_rows[...].astype(BF16).reshape(back_src.shape)
-    back_dst[pl.ds(t, 1)] = back_src[pl.ds(t, 1)]
-    send_table(back_src, back_dst, 6)
 
     wait_all(neg_back_dst, N_TABLE - 1, 5)
     slab_negs[...] = neg_back_dst[...].astype(F32)
@@ -350,8 +362,9 @@
     wait_sent(shard_src, N_DP - 1, 7)
     wait_all(shard_dst, N_DP - 1, 7)
     summed = jnp.sum(shard_dst[...].astype(F32), axis=0)
-    grad_ref[:half, :] = summed[:, : LANES // 2]
-    grad_ref[half:, :] = pltpu.roll(summed, LANES // 2, 1)[:, : LANES // 2]
+    turned = jnp.transpose(summed)
+    grad_ref[:, :half] = turned[: LANES // 2, :]
+    grad_ref[:, half:] = turned[LANES // 2 :, :]
 
 
 def body(
@@ -364,18 +377,20 @@
     history_lengths,
 ):
     vmem = pl.BlockSpec(memory_space=pltpu.VMEM)
-    smem = pl.BlockSpec(memory_space=pltpu.SMEM)
     anywhere = pl.BlockSpec(memory_space=pl.ANY)
     loss, grad = pl.pallas_call(
         kernel,
         name="hstu_step",
         out_shape=(
             jax.ShapeDtypeStruct((1, TOK), F32),
-            jax.ShapeDtypeStruct((OWN_ITEMS, D // N_DP), F32),
+            jax.ShapeDtypeStruct((D // N_DP, OWN_ITEMS), F32),
         ),
-        in_specs=[anywhere, anywhere, anywhere, vmem, vmem, vmem, smem],
+        in_specs=[anywhere] * 7,
         out_specs=(vmem, vmem),
         scratch_shapes=[
+            pltpu.VMEM((8, N_TABLE), jnp.int32),
+            pltpu.VMEM((1, TOK), jnp.int32),
+            pltpu.SMEM((1, SEQS), jnp.int32),
             pltpu.VMEM((OWN_ITEMS, D), BF16),
             pltpu.VMEM((D, 4 * D), BF16),
             pltpu.VMEM((D, D), BF16),
@@ -399,23 +414,23 @@
             pltpu.VMEM((N_TABLE, CHUNKS, LANES), BF16),
             pltpu.VMEM((N_DP, OWN_ITEMS // 2, LANES), BF16),
             pltpu.VMEM((N_DP, OWN_ITEMS // 2, LANES), BF16),
-            pltpu.SemaphoreType.DMA((3,)),
+            pltpu.SemaphoreType.DMA((7,)),
             pltpu.SemaphoreType.DMA((8,)),
             pltpu.SemaphoreType.DMA((8,)),
         ],
         compiler_params=pltpu.CompilerParams(
-            collective_id=0, has_side_effects=True, vmem_limit_bytes=48 * 2**20
+            collective_id=0, has_side_effects=True, vmem_limit_bytes=60 * 2**20
         ),
     )(
+        jnp.transpose(request_rows[0]),
+        jnp.transpose(negative_rows[0]),
+        token_slots,
         item_table,
         input_weight,
         output_weight,
-        request_rows,
-        negative_rows,
-        token_slots,
         history_lengths,
     )
-    return loss.reshape(TOK), grad
+    return loss.reshape(TOK), jnp.transpose(grad)
 
 
 def solution(mesh):

time: 89.2 us -> 77.2 us (0.87)
  Pallas kernels: 80.7 us -> 73.8 us
  local copies, waits for them, and re-layouts: 7.63 us -> 2.59 us
    pallas_call x1, Pallas kernels: 80.7 us -> 73.8 us  [body(): pl.pallas_call(kernel, name='hstu_step', out_shape=(jax.ShapeDtypeStruct(...]
    unnamed x14 -> x2, local copies, waits for them, and re-layouts: 7.63 us -> 2.59 us
where the time goes in v2:
time: 77.2 us; the launch traced here: 77 us
  Pallas kernels  73.8 us (96%)
  local copies, waits for them, and re-layouts  2.59 us (3%)
    pallas_call x1, Pallas kernels, body(): pl.pallas_call(kernel, name='hstu_step', out_shape=(jax.ShapeDtypeStruct(...  73.8 us
    unnamed x2, local copies, waits for them, and re-layouts  2.59 us

profile of v2, /device:TPU:1, one launch (start us, length us, event | category | flops | bytes accessed | tf_op | source)
XLA Modules:
  0.0 77.0 jit_solution(16075942170036211657)
XLA Ops:
  0.6 73.8 %hstu_step.1 = (f32[1,128]{1,0:T(1,128)}, f32[64,256]{1,0:T(8,128)}) custom-call(s32[4,64]{1,0:T(4,128)} %bitcast.7, s32[1,64]{1,0:T(1,128)} %bitcast.8, s32[1,128]{1,0:T(1,128)} %token_hbm.1, bf16[256,512]{1,0:T(8,128)(2,1)} %table_hbm.1, bf16[512,2048]{1,0:T(8,128)(2,1)} %in_weight_hbm.1, bf16[512,512]{1,0:T(8,128)(2,1)} %out_weight_hbm.1, s32[1,4]{1,0:T(1,128)} %length_hbm.1), custom_call_target="tpu_custom_call" | custom-call | tf_op jit(solution)/shard_map/hstu_step/pallas_call | solution.py:381
  74.4 1.1 %copy.11 = f32[128]{0:T(128)} copy(f32[128]{0:T(128)} %bitcast.9) | data formatting | bytes 1024
  75.5 1.5 %copy.12 = f32[256,64]{0,1:T(8,128)} copy(f32[256,64]{0,1:T(8,128)} %bitcast.6) | data formatting | bytes 131072

commit v3 on v2

--- a/solution.py
+++ b/solution.py
@@ -28,9 +28,15 @@
 
 
 OFFSETS = sorted(
-    ((x, z) for x in range(X_RING) for z in range(Z_RING) if x or z),
+    ((x, z) for x in range(X_RING) for z in range(Z_RING)),
     key=lambda o: -(min(o[0], X_RING - o[0]) + min(o[1], Z_RING - o[1])),
 )
+BACK = [OFFSETS.index(((-x) % X_RING, (-z) % Z_RING)) for x, z in OFFSETS]
+SELF = N_TABLE - 1
+DP_ORDER = (4, 5, 2, 3, 6, 7, 1)
+BACK_FAR = 24
+FRONT_NEGS = 63
+FRONT_ROWS = 0
 
 
 def dot(a, b, contract=((1,), (0,))):
@@ -38,22 +44,23 @@
 
 
 def rows_to_slabs(value, slab, slots):
+    size = slots * CHUNKS
     for s in range(slots):
         for c in range(CHUNKS):
-            slab[pl.ds(s * CHUNKS + c, N_TABLE, stride=slots * CHUNKS), :] = value[
+            slab[pl.ds(s * CHUNKS + c, N_TABLE, stride=size), :] = value[
                 s * N_TABLE : (s + 1) * N_TABLE, c * LANES : (c + 1) * LANES
             ]
 
 
 def slabs_to_rows(slab, slots):
+    size = slots * CHUNKS
     rows = []
     for s in range(slots):
         parts = [
-            slab[pl.ds(s * CHUNKS + c, N_TABLE, stride=slots * CHUNKS), :]
-            for c in range(CHUNKS)
+            slab[pl.ds(s * CHUNKS + c, N_TABLE, stride=size), :] for c in range(CHUNKS)
         ]
         rows.append(jnp.concatenate(parts, axis=1))
-    return rows[0] if slots == 1 else jnp.concatenate(rows, axis=0)
+    return rows
 
 
 def center_parts(values):
@@ -144,21 +151,19 @@
 
     barrier = pltpu.get_barrier_semaphore()
 
-    for offset in OFFSETS:
+    for offset in OFFSETS[:SELF]:
         pl.semaphore_signal(
             barrier, inc=1, device_id={"table": table_peer(offset)}, device_id_type=MESH
         )
-    for k in range(1, N_DP):
-        pl.semaphore_signal(
-            barrier, inc=1, device_id={"dp": lax.rem(i + k, N_DP)}, device_id_type=MESH
-        )
-
-    def send_table(src, dst, n):
-        for offset in OFFSETS:
-            peer = table_peer(offset)
+    for k in DP_ORDER:
+        pl.semaphore_signal(barrier, inc=1, device_id={"dp": i ^ k}, device_id_type=MESH)
+
+    def send_table(src_of, dst_of, n, first=0, count=SELF):
+        for k in range(first, min(first + count, SELF)):
+            peer = table_peer(OFFSETS[k])
             pltpu.make_async_remote_copy(
-                src_ref=src.at[peer],
-                dst_ref=dst.at[t],
+                src_ref=src_of(k, peer),
+                dst_ref=dst_of(k),
                 send_sem=send_sem.at[n],
                 recv_sem=recv_sem.at[n],
                 device_id={"table": peer},
@@ -166,8 +171,8 @@
             ).start()
 
     def send_dp(src_of, dst, n):
-        for k in range(1, N_DP):
-            peer = lax.rem(i + k, N_DP)
+        for k in DP_ORDER:
+            peer = i ^ k
             pltpu.make_async_remote_copy(
                 src_ref=src_of(peer),
                 dst_ref=dst,
@@ -191,9 +196,9 @@
         [request_v[0 : CAP + 1, :], jnp.zeros((LANES - CAP - 1, N_TABLE), jnp.int32)], axis=0
     )
     ask_src[:, 0, :] = jnp.transpose(asks.astype(F32)).astype(jnp.int32)
-    ask_dst[pl.ds(t, 1)] = ask_src[pl.ds(t, 1)]
+    ask_dst[pl.ds(SELF, 1)] = ask_src[pl.ds(t, 1)]
     pl.semaphore_wait(barrier, N_TABLE - 1 + N_DP - 1)
-    send_table(ask_src, ask_dst, 0)
+    send_table(lambda k, peer: ask_src.at[peer], lambda k: ask_dst.at[BACK[k]], 0)
 
     sub_tok = lax.broadcasted_iota(jnp.int32, (TOK, TOK), 0)
     lane_tok = lax.broadcasted_iota(jnp.int32, (TOK, TOK), 1)
@@ -219,24 +224,29 @@
     token_t = token_t.astype(BF16)
 
     loads[3].wait()
-    wait_all(ask_dst, N_TABLE - 1, 0)
+    wait_all(ask_dst, SELF, 0)
     asked = ask_dst[:, 0, :]
     item = lax.broadcasted_iota(jnp.int32, (N_TABLE, OWN_ITEMS), 1)
     for s in range(CAP + 1):
         picks[s * N_TABLE : (s + 1) * N_TABLE, :] = (
-            (asked[:, s : s + 1] == item).astype(F32).astype(BF16)
-        )
-    own_table = table_v[...]
-    found_negs = dot(picks[CAP * N_TABLE :, :], own_table)
+            (asked[:, s : s + 1] == item).astype(F32)
+        ).astype(BF16)
+    found = dot(picks[...], table_v[...])
     for c in range(CHUNKS):
-        slab_negs[:, c, :] = found_negs[:, c * LANES : (c + 1) * LANES]
+        slab_negs[:, c, :] = found[CAP * N_TABLE :, c * LANES : (c + 1) * LANES]
     neg_src[...] = slab_negs[...].astype(BF16)
-    neg_dst[pl.ds(t, 1)] = neg_src[pl.ds(t, 1)]
-    send_table(neg_src, neg_dst, 1)
-    rows_to_slabs(dot(picks[: CAP * N_TABLE, :], own_table), slab_rows, CAP)
+    negs_out = lambda k, peer: neg_src.at[k]
+    negs_at = lambda k: neg_dst.at[t]
+    send_table(negs_out, negs_at, 1, 0, FRONT_NEGS)
+    rows_to_slabs(found, slab_rows, CAP)
     row_src[...] = slab_rows[...].astype(BF16).reshape(row_src.shape)
-    row_dst[pl.ds(t, 1)] = row_src[pl.ds(t, 1)]
-    send_table(row_src, row_dst, 2)
+    rows_out = lambda k, peer: row_src.at[k]
+    rows_at = lambda k: row_dst.at[t]
+    send_table(rows_out, rows_at, 2, 0, FRONT_ROWS)
+    send_table(negs_out, negs_at, 1, FRONT_NEGS)
+    send_table(rows_out, rows_at, 2, FRONT_ROWS)
+    neg_dst[pl.ds(t, 1)] = neg_src[pl.ds(SELF, 1)]
+    row_dst[pl.ds(t, 1)] = row_src[pl.ds(SELF, 1)]
     picks_t[...] = jnp.transpose(picks[...].astype(F32)).astype(BF16)
 
     wait_all(neg_dst, N_TABLE - 1, 1)
@@ -250,7 +260,7 @@
 
     wait_all(row_dst, N_TABLE - 1, 2)
     slab_rows[...] = row_dst[...].reshape(slab_rows.shape).astype(F32)
-    history = slabs_to_rows(slab_rows, CAP).astype(BF16)
+    history = jnp.concatenate(slabs_to_rows(slab_rows, CAP), axis=0).astype(BF16)
     inputs = dot(token_pick, history)
     normed, in_scale = center_parts(inputs)
     pre = dot(normed.astype(BF16), in_weight[...])
@@ -319,8 +329,10 @@
 
     rows_to_slabs(dot(token_t, d_inputs.astype(BF16)), slab_rows, CAP)
     back_src[...] = slab_rows[...].astype(BF16).reshape(back_src.shape)
-    back_dst[pl.ds(t, 1)] = back_src[pl.ds(t, 1)]
-    send_table(back_src, back_dst, 6)
+    back_dst[pl.ds(SELF, 1)] = back_src[pl.ds(t, 1)]
+    rows_back = lambda k, peer: back_src.at[peer]
+    rows_to = lambda k: back_dst.at[BACK[k]]
+    send_table(rows_back, rows_to, 6, 0, BACK_FAR)
 
     wait_all(neg_in, N_DP - 1, 4)
     d_units = jnp.sum(neg_in[...].astype(F32), axis=0)
@@ -329,17 +341,19 @@
     for c in range(CHUNKS):
         slab_negs[:, c, :] = d_negs[:, c * LANES : (c + 1) * LANES]
     neg_back_src[...] = slab_negs[...].astype(BF16)
-    neg_back_dst[pl.ds(t, 1)] = neg_back_src[pl.ds(t, 1)]
-    send_table(neg_back_src, neg_back_dst, 5)
+    neg_back_dst[pl.ds(SELF, 1)] = neg_back_src[pl.ds(t, 1)]
+    negs_back = lambda k, peer: neg_back_src.at[peer]
+    negs_to = lambda k: neg_back_dst.at[BACK[k]]
+    send_table(negs_back, negs_to, 5)
+    send_table(rows_back, rows_to, 6, BACK_FAR)
 
     wait_all(neg_back_dst, N_TABLE - 1, 5)
     slab_negs[...] = neg_back_dst[...].astype(F32)
     back_negs = jnp.concatenate([slab_negs[:, c, :] for c in range(CHUNKS)], axis=1)
-    shard_negs = dot(picks_t[:, CAP * N_TABLE :], back_negs.astype(BF16))
     wait_all(back_dst, N_TABLE - 1, 6)
     slab_rows[...] = back_dst[...].reshape(slab_rows.shape).astype(F32)
-    back_rows = slabs_to_rows(slab_rows, CAP).astype(BF16)
-    shard = shard_negs + dot(picks_t[:, : CAP * N_TABLE], back_rows)
+    back = slabs_to_rows(slab_rows, CAP) + [back_negs]
+    shard = dot(picks_t[...], jnp.concatenate(back, axis=0).astype(BF16))
 
     half = OWN_ITEMS // 2
     left = lax.broadcasted_iota(jnp.int32, (half, LANES), 1) < LANES // 2

time: 77.2 us -> 74.6 us (0.966)
  Pallas kernels: 73.8 us -> 71.2 us
    pallas_call x1, Pallas kernels: 73.8 us -> 71.2 us  [body(): pl.pallas_call(kernel, name='hstu_step', out_shape=(jax.ShapeDtypeStruct(...]
where the time goes in v3:
time: 74.6 us; the launch traced here: 74.4 us
  Pallas kernels  71.2 us (95%)
  local copies, waits for them, and re-layouts  2.59 us (3%)
    pallas_call x1, Pallas kernels, body(): pl.pallas_call(kernel, name='hstu_step', out_shape=(jax.ShapeDtypeStruct(...  71.2 us
    unnamed x2, local copies, waits for them, and re-layouts  2.59 us

profile of v3, /device:TPU:1, one launch (start us, length us, event | category | flops | bytes accessed | tf_op | source)
XLA Modules:
  0.0 74.4 jit_solution(7105117470626599722)
XLA Ops:
  0.6 71.2 %hstu_step.1 = (f32[1,128]{1,0:T(1,128)}, f32[64,256]{1,0:T(8,128)}) custom-call(s32[4,64]{1,0:T(4,128)} %bitcast.7, s32[1,64]{1,0:T(1,128)} %bitcast.8, s32[1,128]{1,0:T(1,128)} %token_hbm.1, bf16[256,512]{1,0:T(8,128)(2,1)} %table_hbm.1, bf16[512,2048]{1,0:T(8,128)(2,1)} %in_weight_hbm.1, bf16[512,512]{1,0:T(8,128)(2,1)} %out_weight_hbm.1, s32[1,4]{1,0:T(1,128)} %length_hbm.1), custom_call_target="tpu_custom_call" | custom-call | tf_op jit(solution)/shard_map/hstu_step/pallas_call | solution.py:395
  71.8 1.1 %copy.11 = f32[128]{0:T(128)} copy(f32[128]{0:T(128)} %bitcast.9) | data formatting | bytes 1024
  72.9 1.5 %copy.12 = f32[256,64]{0,1:T(8,128)} copy(f32[256,64]{0,1:T(8,128)} %bitcast.6) | data formatting | bytes 131072

commit v4 on v3

--- a/solution.py
+++ b/solution.py
@@ -86,18 +86,13 @@
 
 
 def kernel(
-    request_hbm,
-    negative_hbm,
-    token_hbm,
+    small_hbm,
     table_hbm,
     in_weight_hbm,
     out_weight_hbm,
-    length_hbm,
     loss_ref,
     grad_ref,
-    request_v,
-    token_v,
-    length_ref,
+    small,
     table_v,
     in_weight,
     out_weight,
@@ -136,13 +131,10 @@
         pltpu.make_async_copy(src, dst, local_sem.at[n])
         for n, (src, dst) in enumerate(
             (
-                (request_hbm, request_v.at[pl.ds(0, CAP)]),
-                (negative_hbm, request_v.at[pl.ds(CAP, 1)]),
-                (token_hbm, token_v),
+                (small_hbm, small),
                 (table_hbm, table_v),
                 (in_weight_hbm, in_weight),
                 (out_weight_hbm, out_weight),
-                (length_hbm, length_ref),
             )
         )
     ]
@@ -191,31 +183,26 @@
         pltpu.make_async_copy(part, part, send_sem.at[n]).wait()
 
     loads[0].wait()
-    loads[1].wait()
-    asks = jnp.concatenate(
-        [request_v[0 : CAP + 1, :], jnp.zeros((LANES - CAP - 1, N_TABLE), jnp.int32)], axis=0
-    )
-    ask_src[:, 0, :] = jnp.transpose(asks.astype(F32)).astype(jnp.int32)
+    asks = jnp.concatenate([small[...], jnp.zeros((LANES - 8, LANES), jnp.int32)], axis=0)
+    ask_src[:, 0, :] = jnp.transpose(asks.astype(F32))[:N_TABLE, :].astype(jnp.int32)
     ask_dst[pl.ds(SELF, 1)] = ask_src[pl.ds(t, 1)]
     pl.semaphore_wait(barrier, N_TABLE - 1 + N_DP - 1)
     send_table(lambda k, peer: ask_src.at[peer], lambda k: ask_dst.at[BACK[k]], 0)
 
     sub_tok = lax.broadcasted_iota(jnp.int32, (TOK, TOK), 0)
     lane_tok = lax.broadcasted_iota(jnp.int32, (TOK, TOK), 1)
-    loads[6].wait()
     seg_q = jnp.zeros((TOK, TOK), jnp.int32)
     seg_k = jnp.zeros((TOK, TOK), jnp.int32)
     seg_next = jnp.zeros((TOK, TOK), jnp.int32)
-    end = jnp.int32(0)
-    for n in range(length_ref.shape[1]):
-        end = end + length_ref[0, n]
+    end = jnp.zeros((1, 1), jnp.int32)
+    for n in range(SEQS):
+        end = end + small[CAP + 2 : CAP + 3, n : n + 1]
         seg_q = seg_q + (sub_tok >= end).astype(jnp.int32)
         seg_k = seg_k + (lane_tok >= end).astype(jnp.int32)
         seg_next = seg_next + (sub_tok + 1 >= end).astype(jnp.int32)
     allowed = (seg_q == seg_k) & (lane_tok <= sub_tok)
     valid = ((seg_q == seg_next) & (sub_tok < TOK - 1))[:, 0:1]
-    loads[2].wait()
-    slots = token_v[...]
+    slots = small[CAP + 1 : CAP + 2, :]
     place = (slots & (CAP - 1)) * N_TABLE + slots // CAP
     token_t = (
         lax.broadcasted_iota(jnp.int32, (CAP * N_TABLE, TOK), 0) == place
@@ -223,7 +210,7 @@
     token_pick = jnp.transpose(token_t).astype(BF16)
     token_t = token_t.astype(BF16)
 
-    loads[3].wait()
+    loads[1].wait()
     wait_all(ask_dst, SELF, 0)
     asked = ask_dst[:, 0, :]
     item = lax.broadcasted_iota(jnp.int32, (N_TABLE, OWN_ITEMS), 1)
@@ -255,8 +242,8 @@
     neg_raw[...] = negs
     unit_all[pl.ds(i, 1)] = (negs * unit_scale(negs)).astype(BF16)[None]
     send_dp(lambda peer: unit_all.at[i], unit_all.at[i], 3)
-    loads[4].wait()
-    loads[5].wait()
+    loads[2].wait()
+    loads[3].wait()
 
     wait_all(row_dst, N_TABLE - 1, 2)
     slab_rows[...] = row_dst[...].reshape(slab_rows.shape).astype(F32)
@@ -392,6 +379,17 @@
 ):
     vmem = pl.BlockSpec(memory_space=pltpu.VMEM)
     anywhere = pl.BlockSpec(memory_space=pl.ANY)
+    small = jnp.zeros((8, LANES), jnp.int32)
+    first = 0
+    for line in (
+        jnp.transpose(request_rows[0]),
+        jnp.transpose(negative_rows[0]),
+        token_slots,
+        history_lengths,
+    ):
+        rows, width = line.shape
+        small = small + jnp.pad(line, ((first, 8 - first - rows), (0, LANES - width)))
+        first += rows
     loss, grad = pl.pallas_call(
         kernel,
         name="hstu_step",
@@ -399,12 +397,10 @@
             jax.ShapeDtypeStruct((1, TOK), F32),
             jax.ShapeDtypeStruct((D // N_DP, OWN_ITEMS), F32),
         ),
-        in_specs=[anywhere] * 7,
+        in_specs=[anywhere] * 4,
         out_specs=(vmem, vmem),
         scratch_shapes=[
-            pltpu.VMEM((8, N_TABLE), jnp.int32),
-            pltpu.VMEM((1, TOK), jnp.int32),
-            pltpu.SMEM((1, SEQS), jnp.int32),
+            pltpu.VMEM((8, LANES), jnp.int32),
             pltpu.VMEM((OWN_ITEMS, D), BF16),
             pltpu.VMEM((D, 4 * D), BF16),
             pltpu.VMEM((D, D), BF16),
@@ -428,21 +424,18 @@
             pltpu.VMEM((N_TABLE, CHUNKS, LANES), BF16),
             pltpu.VMEM((N_DP, OWN_ITEMS // 2, LANES), BF16),
             pltpu.VMEM((N_DP, OWN_ITEMS // 2, LANES), BF16),
-            pltpu.SemaphoreType.DMA((7,)),
+            pltpu.SemaphoreType.DMA((4,)),
             pltpu.SemaphoreType.DMA((8,)),
             pltpu.SemaphoreType.DMA((8,)),
         ],
         compiler_params=pltpu.CompilerParams(
-            collective_id=0, has_side_effects=True, vmem_limit_bytes=60 * 2**20
+            collective_id=0, has_side_effects=True, vmem_limit_bytes=215 * 2**18
         ),
     )(
-        jnp.transpose(request_rows[0]),
-        jnp.transpose(negative_rows[0]),
-        token_slots,
+        small,
         item_table,
         input_weight,
         output_weight,
-        history_lengths,
     )
     return loss.reshape(TOK), jnp.transpose(grad)
 

time: 74.6 us -> 73.3 us (0.983)
  local copies, waits for them, and re-layouts: 2.59 us -> 1.14 us
    unnamed x2, local copies, waits for them, and re-layouts: 2.59 us -> 1.14 us
where the time goes in v4:
time: 73.3 us; the launch traced here: 73.1 us
  Pallas kernels  70.6 us (96%)
  local copies, waits for them, and re-layouts  1.14 us (2%)
  other arithmetic  0.74 us (1%)
    pallas_call x1, Pallas kernels, body(): pl.pallas_call(kernel, name='hstu_step', out_shape=(jax.ShapeDtypeStruct(...  70.6 us

profile of v4, /device:TPU:1, one launch (start us, length us, event | category | flops | bytes accessed | tf_op | source)
XLA Modules:
  0.0 73.1 jit_solution(9122014025087387108)
XLA Ops:
  0.6 0.7 %pad_add_fusion.small_hbm = s32[8,128]{1,0:T(8,128)S(1)} fusion(s32[1,4]{1,0:T(1,128)} %param.13, s32[1,128]{1,0:T(1,128)} %param.12, s32[1,64]{1,0:T(1,128)} %bitcast.9, s32[4,64]{1,0:T(4,128)} %bitcast.8), kind=kLoop, calls=%fused_computation | loop fusion | flops 3072 | bytes 5904 | tf_op jit(solution)/shard_map/add | solution.py:391
  1.4 70.6 %hstu_step.1 = (f32[1,128]{1,0:T(1,128)S(1)}, f32[64,256]{1,0:T(8,128)S(1)}) custom-call(s32[8,128]{1,0:T(8,128)S(1)} %pad_add_fusion.small_hbm, bf16[256,512]{1,0:T(8,128)(2,1)} %table_hbm.1, bf16[512,2048]{1,0:T(8,128)(2,1)} %in_weight_hbm.1, bf16[512,512]{1,0:T(8,128)(2,1)} %out_weight_hbm.1), custom_call_target="tpu_custom_call" | custom-call | tf_op jit(solution)/shard_map/hstu_step/pallas_call | solution.py:393
  72.0 0.5 copy.11
  72.5 0.6 copy.12
